TPU v7x, 32 devices: a whole 2x2x4 slice. The times are simulated.
32 devices in a mesh: seq: 8 (over y, x, core), head: 4 (over z).
Axes of the slice: x: 2, y: 2, z: 4, core: 2. Of those that a mesh axis runs over, the one named last changes fastest.
Arguments:
- queries: bfloat16 [512, 8192], P('seq', 'head'), may hold values from -6 to 6
- keys: bfloat16 [512, 1024], P('seq'), may hold values from -6 to 6
- values: bfloat16 [512, 1024], P('seq'), may hold values from -6 to 6
- vertical: int32 [64, 8], replicated, may hold values from -1 to 7, as said below
- slash: int32 [64, 8], replicated, may hold values from -1 to 7, as said below
- plan: int32 [64], replicated, may hold values from 0 to 63, each once
Outputs:
- attended: bfloat16 [512, 8192], P('seq', 'head')
Inputs may be any that keep to these rules, and one draw needn't show every extreme that they name: `vertical`: entries of 0 or more name key blocks of 64 positions; -1 marks an unused entry, and every row has at least one used entry. `slash`: entries of 0 or more are offsets back from a query's own block; -1 marks an unused entry; the first entry of every row is 0. `plan`: A permutation of the query heads.
All inputs are finite; a program needn't handle non-finite values.
Results may differ from a plain program's by a relative error of at most 0.0044.
Values may be sent and summed in bfloat16 or wider, within the bound.
No kernel may reach another device: no remote copies, remote signals or barrier semaphores. Data moves between devices by JAX's collectives and lax.ppermute only.
A program may use at most 64 MiB of HBM per device.

v0:
```python
import functools
import math

import jax
import jax.numpy as jnp
from jax import lax
from jax.experimental import pallas as pl
from jax.experimental.pallas import tpu as pltpu
from jax.sharding import PartitionSpec as P

HD = 128
QH = 64
KVH = 8
BLK = 64
GROUP = QH // KVH
HEADS_AT_ONCE = 4
LANES = 128

floor_value = -1e30

SMEM = pl.BlockSpec(memory_space=pltpu.SMEM)
VMEM = pl.BlockSpec(memory_space=pltpu.VMEM)
ANY = pl.BlockSpec(memory_space=pl.ANY)
SMALL = 1024 * 1024


def shift_of(size):
    assert size & (size - 1) == 0
    return size.bit_length() - 1


def turned(index, size):
    return ((index << 1) | (index >> (shift_of(size) - 1))) & (size - 1)


def entry_bits(table):
    bits = jnp.zeros((1, table.shape[1]), jnp.int32)
    for entry in range(table.shape[0]):
        named = table[entry : entry + 1, :]
        bits = bits | jnp.where(named >= 0, jnp.int32(1) << jnp.maximum(named, 0), 0)
    return bits


class Tally:
    def __init__(self, head_size, held):
        self.width = shift_of(held) + 1
        self.per_word = 31 // self.width
        self.words = [jnp.int32(0)] * -(-head_size // self.per_word)

    def rank_and_count(self, owner):
        if len(self.words) == 1:
            at = owner * self.width
            rank = self.words[0] >> at
            self.words[0] = self.words[0] + (jnp.int32(1) << at)
        else:
            word = owner // self.per_word
            at = (owner - word * self.per_word) * self.width
            held_word = self.words[0]
            for index in range(1, len(self.words)):
                held_word = jnp.where(word == index, self.words[index], held_word)
            rank = held_word >> at
            one = jnp.int32(1) << at
            self.words = [w + jnp.where(word == index, one, 0) for index, w in enumerate(self.words)]
        return rank & ((1 << self.width) - 1)

    def count(self, owner):
        word = self.words[owner // self.per_word]
        return (word >> (owner % self.per_word * self.width)) & ((1 << self.width) - 1)


def route_kernel(head_size, held, levels, plan, vertical, slash, send, slots, level, bits):
    own = lax.axis_index("head")
    most = [jnp.int32(0)] * head_size
    for target in range(head_size):
        tally = Tally(head_size, held)
        for t in range(held):
            head = plan[target * held + t]
            owner = head >> shift_of(held)
            rank = tally.rank_and_count(owner)
            send[jnp.where(owner == own, head & (held - 1), held)] = ((owner ^ target) << shift_of(held)) + rank
        for owner in range(head_size):
            most[owner ^ target] = jnp.maximum(most[owner ^ target], tally.count(owner))
    tally = Tally(head_size, held)
    for distance in range(head_size):
        slots[head_size * held + distance] = 0
    for t in range(held):
        owner = plan[own * held + t] >> shift_of(held)
        rank = tally.rank_and_count(owner)
        distance = owner ^ own
        slots[(distance << shift_of(held)) + rank] = t
        slots[head_size * held + distance] = rank + 1
    chosen = jnp.int32(len(levels) - 1)
    for index in reversed(range(len(levels) - 1)):
        fits = most[1] <= levels[index][1]
        for distance in range(2, head_size):
            fits = fits & (most[distance] <= levels[index][distance])
        chosen = jnp.where(fits, index, chosen)
    level[0] = chosen
    bits[0:1, :] = entry_bits(vertical)
    bits[1:2, :] = entry_bits(slash)


def attention_kernel(
    seq_size, held, kv_heads, send, bits, kv_own, kv_other, query_ref, out_ref, send_here, copied
):
    send_copy = pltpu.make_async_copy(send, send_here, copied)
    send_copy.start()
    query_len = query_ref.shape[0]
    key_len = query_len
    own_seq = lax.axis_index("seq")
    own_head = lax.axis_index("head")
    chips = seq_size // 2
    half = chips * key_len

    piece = lax.broadcasted_iota(jnp.int32, (1, 2 * half), 1) // key_len
    core = jnp.where(piece < chips, own_seq & 1, 1 - (own_seq & 1))
    flip = piece & (chips - 1)
    flip = jnp.where(core == 0, flip, turned(flip, chips))
    block = ((own_seq >> 1) ^ flip) * 2 + core
    back = own_seq - block
    present = back >= 0
    back_shift = jnp.maximum(back, 0)
    heads = own_head * held + lax.broadcasted_iota(jnp.int32, (held, bits.shape[1]), 0)
    is_head = lax.broadcasted_iota(jnp.int32, (held, bits.shape[1]), 1) == heads
    vertical_bits, slash_bits = (
        jnp.sum(jnp.where(is_head, bits[kind : kind + 1, :], 0), axis=1, keepdims=True) for kind in range(2)
    )
    hit = ((vertical_bits >> block) | (slash_bits >> back_shift)) & 1
    bias = jnp.where((hit == 1) & present, 0.0, floor_value)
    row = lax.broadcasted_iota(jnp.int32, (query_len, LANES), 0)
    column = lax.broadcasted_iota(jnp.int32, (query_len, LANES), 1)
    causal = (column <= row) | (column >= key_len)
    score_scale = HD ** (-0.5) * math.log2(math.e)
    per_kv = held // kv_heads

    def scores_of(lead):
        heads = range(lead, min(lead + HEADS_AT_ONCE, held))
        key_at = lead // per_kv * HD
        key = jnp.concatenate([kv_own[:, key_at : key_at + HD], kv_other[:, key_at : key_at + HD]], axis=0)
        query = jnp.concatenate([query_ref[:, i * HD : (i + 1) * HD] for i in heads], axis=0)
        return lax.dot_general(
            query, key, (((1,), (1,)), ((), ())), preferred_element_type=jnp.float32
        )

    following = scores_of(0)
    for lead in range(0, held, HEADS_AT_ONCE):
        heads = range(lead, min(lead + HEADS_AT_ONCE, held))
        scores = following
        if lead + HEADS_AT_ONCE < held:
            following = scores_of(lead + HEADS_AT_ONCE)
        value_at = (lead // per_kv + kv_heads) * HD
        value = jnp.concatenate(
            [kv_own[:, value_at : value_at + HD], kv_other[:, value_at : value_at + HD]], axis=0
        )
        weights = []
        totals = []
        for at, i in enumerate(heads):
            masked = scores[at * query_len : (at + 1) * query_len] + bias[i : i + 1, :]
            masked = jnp.concatenate(
                [jnp.where(causal, masked[:, :LANES], floor_value), masked[:, LANES:]], axis=1
            )
            row_max = jnp.max(masked, axis=1, keepdims=True)
            weight = jnp.exp2((masked - row_max) * score_scale)
            totals.append(1.0 / jnp.sum(weight, axis=1, keepdims=True))
            weights.append(weight.astype(jnp.bfloat16))
        mixture = jnp.dot(
            jnp.concatenate(weights, axis=0), value, preferred_element_type=jnp.float32
        )
        if lead == 0:
            send_copy.wait()
        for at, i in enumerate(heads):
            mix = mixture[at * query_len : (at + 1) * query_len]
            out_ref[send_here[i]] = (mix * totals[at]).astype(out_ref.dtype)


def place_kernel(head_size, held, ops, slots, *refs):
    out_ref, done = refs[-2:]
    odd = lax.axis_index("seq") & 1
    for (size, parts), ref in zip(ops, refs):
        distance, first, least = (jnp.where(odd == 0, *choice) for choice in zip(*parts))
        arriving = slots[head_size * held + distance]
        for index in range(size):
            rank = first + index

            @pl.when((rank >= least) & (rank < arriving))
            def _(ref=ref, rank=rank, index=index, distance=distance):
                at = pl.multiple_of(slots[distance * held + rank] * HD, HD)
                pltpu.make_async_copy(ref.at[index], out_ref.at[:, pl.ds(at, HD)], done).start()

    pltpu.make_async_copy(out_ref, out_ref, done).wait()


def capacity_levels(head_size, held):
    steps = sorted({max(1, held * c // 16) for c in (4, 5, 6, 7, 8)})
    fars = sorted(((b, c) for b in steps for c in steps), key=sum)
    fars += [(max(1, held * 10 // 16),) * 2, (held,) * 2]
    return [
        tuple(min(held, sum(far)) if m < head_size // 2 else far[m % 2] for m in range(head_size))
        for far in fars
    ]


def exchange_ops(head_size, held, capacities):
    if head_size != 4:
        return [(capacities[m], ((m, 0, 0),) * 2) for m in range(1, head_size)]
    b, c = capacities[2:]
    near, rest = (1, 0, 0), (1, min(b, held - c), b)
    middle, far = (2, 0, 0), (3, 0, 0)
    return [(c, (far, rest)), (b, (middle, near)), (c, (rest, far)), (b, (near, middle))]


def exchange(head_size, held, capacities, packed, slots):
    seq_size = lax.axis_size("seq")
    odd = lax.axis_index("seq") & 1
    ops = exchange_ops(head_size, held, capacities)
    arrived = []
    for size, parts in ops:
        even_at, odd_at = (distance * held + first for distance, first, _ in parts)
        pairs = [
            (i * head_size + z, i * head_size + (z ^ parts[i & 1][0]))
            for i in range(seq_size)
            for z in range(head_size)
        ]
        heads = lax.dynamic_slice_in_dim(packed, jnp.where(odd == 0, even_at, odd_at), size, axis=0)
        arrived.append(lax.ppermute(heads, ("seq", "head"), pairs))
    kept = (held, ((0, 0, 0),) * 2)
    return pl.pallas_call(
        functools.partial(place_kernel, head_size, held, [kept] + ops),
        out_shape=pltpu.HBM((packed.shape[1], held * HD), packed.dtype),
        in_specs=[SMEM] + [ANY] * (1 + len(ops)),
        out_specs=pl.BlockSpec(memory_space=pltpu.HBM),
        scratch_shapes=[pltpu.SemaphoreType.DMA],
        compiler_params=pltpu.CompilerParams(vmem_limit_bytes=SMALL),
        name="place",
    )(slots, packed, *arrived)


def per_device(queries, keys, values, vertical, slash, plan):
    seq_size = lax.axis_size("seq")
    head_size = lax.axis_size("head")
    query_len = queries.shape[0]
    held = queries.shape[1] // HD
    kv_heads = max(1, held // GROUP)
    chips = seq_size // 2
    assert query_len == BLK and plan.shape[0] == held * head_size and chips & (chips - 1) == 0

    levels = capacity_levels(head_size, held)
    send, slots, level, bits = pl.pallas_call(
        functools.partial(route_kernel, head_size, held, levels),
        out_shape=[
            jax.ShapeDtypeStruct((held + 1,), jnp.int32),
            jax.ShapeDtypeStruct((head_size * held + head_size,), jnp.int32),
            jax.ShapeDtypeStruct((1,), jnp.int32),
            jax.ShapeDtypeStruct((2, vertical.shape[0]), jnp.int32),
        ],
        in_specs=[SMEM, VMEM, VMEM],
        out_specs=[SMEM] * 3 + [VMEM],
        compiler_params=pltpu.CompilerParams(vmem_limit_bytes=SMALL),
        name="route",
    )(plan, vertical.T, slash.T)

    kv_at = lax.axis_index("head") * held // GROUP * HD
    kv = jnp.concatenate(
        [lax.dynamic_slice_in_dim(rows, kv_at, kv_heads * HD, axis=1) for rows in (keys, values)], axis=1
    )
    pieces = [kv]
    for m in range(1, chips):
        flips = (2 * m, 2 * turned(m, chips))
        pieces.append(lax.ppermute(kv, "seq", [(i, i ^ flips[i & 1]) for i in range(seq_size)]))
    pieces, send, slots, level, bits = lax.optimization_barrier((pieces, send, slots, level, bits))
    kv_own = jnp.concatenate(pieces, axis=0)
    kv_other = lax.ppermute(kv_own, "seq", [(i, i ^ 1) for i in range(seq_size)])

    packed = pl.pallas_call(
        functools.partial(attention_kernel, seq_size, held, kv_heads),
        out_shape=jax.ShapeDtypeStruct((head_size * held, query_len, HD), jnp.bfloat16),
        in_specs=[ANY] + [VMEM] * 4,
        out_specs=VMEM,
        scratch_shapes=[pltpu.SMEM(send.shape, send.dtype), pltpu.SemaphoreType.DMA],
        compiler_params=pltpu.CompilerParams(vmem_limit_bytes=40 * 1024 * 1024),
        name="attention",
    )(send, bits, kv_own, kv_other, queries)

    return lax.switch(
        level[0],
        [functools.partial(exchange, head_size, held, capacities) for capacities in levels],
        packed,
        slots,
    )


def solution(mesh):
    in_specs = (P("seq", "head"), P("seq", None), P("seq", None), P(), P(), P())
    out_specs = P("seq", "head")
    return jax.shard_map(
        per_device, mesh=mesh, in_specs=in_specs, out_specs=out_specs, check_vma=False
    )
```

profile of v0, /device:TPU:0, one launch (start us, length us, event | category | flops | bytes accessed | tf_op | source)
XLA Modules:
  0.0 27.5 jit_solution(17690924561967400491)
XLA Ops:
  0.0 0.8 %constant_dynamic-slice_fusion.108 = (bf16[64,256]{1,0:T(8,128)(2,1)S(1)}, bf16[64,256]{1,0:T(8,128)(2,1)S(1)}) fusion(bf16[64,1024]{1,0:T(8,128)(2,1)} %param.35, s32[]{:T(128)S(6)} %select_n.443, bf16[64,1024]{1,0:T(8,128)(2,1)} %param.34), kind=kLoop, calls=%fused_computation.113 | loop fusion | bytes 131076 | tf_op jit(solution)/shard_map/dynamic_slice | solution.py:264
  0.8 0.0 copy-start.1
  0.8 0.0 copy-start.2
  0.8 4.0 %collective-permute-start.110 = (bf16[64,512]{1,0:T(8,128)(2,1)S(1)}, bf16[64,512]{1,0:T(8,128)(2,1)S(1)}, u32[]{:S(2)}, u32[]{:S(2)}) collective-permute-start(bf16[64,512]{1,0:T(8,128)(2,1)S(1)} %pad_maximum_fusion), channel_id=1, source_target_pairs={{0,24},{4,28},{8,16},{12,20},{16,8},{20,12},{24,0},{28,4},{1,25},{... | collective-permute-start | bytes 196616 | tf_op jit(solution)/shard_map/ppermute | solution.py:269
  4.8 0.5 %collective-permute-start.109 = (bf16[64,512]{1,0:T(8,128)(2,1)S(1)}, bf16[64,512]{1,0:T(8,128)(2,1)S(1)}, u32[]{:S(2)}, u32[]{:S(2)}) collective-permute-start(bf16[64,512]{1,0:T(8,128)(2,1)S(1)} %pad_maximum_fusion), channel_id=1, source_target_pairs={{0,16},{4,12},{8,24},{12,4},{16,0},{20,28},{24,8},{28,20},{1,17},{... | collective-permute-start | bytes 196616 | tf_op jit(solution)/shard_map/ppermute | solution.py:269
  5.3 0.1 collective-permute-start.108
  5.4 0.0 copy-start.3
  5.4 0.0 copy-done.1
  5.4 0.0 copy-done.2
  5.4 0.6 %copy-done.3 = s32[64]{0:T(128)S(1)} copy-done((s32[64]{0:T(128)S(1)}, s32[64]{0:T(128)}, u32[]{:S(2)}) %copy-start.3) | copy-done | bytes 280
  6.1 1.5 %route.1 = (s32[17]{0:T(128)S(1)}, s32[68]{0:T(128)S(1)}, s32[1]{0:T(128)}, s32[2,64]{1,0:T(2,128)S(1)}) custom-call(s32[64]{0:T(128)S(1)} %copy-done.3, s32[8,64]{1,0:T(8,128)S(1)} %bitcast.3, s32[8,64]{1,0:T(8,128)S(1)} %bitcast.4), custom_call_target="tpu_custom_call" | custom-call | tf_op jit(solution)/shard_map/route/pallas_call | solution.py:248
  7.5 0.0 collective-permute-done.110
  7.6 1.5 %collective-permute-done.109 = bf16[64,512]{1,0:T(8,128)(2,1)S(1)} collective-permute-done((bf16[64,512]{1,0:T(8,128)(2,1)S(1)}, bf16[64,512]{1,0:T(8,128)(2,1)S(1)}, u32[]{:S(2)}, u32[]{:S(2)}) %collective-permute-start.109) | collective-permute-done | bytes 65568 | tf_op jit(solution)/shard_map/ppermute | solution.py:269
  9.0 0.5 %collective-permute-done.108 = bf16[64,512]{1,0:T(8,128)(2,1)S(1)} collective-permute-done((bf16[64,512]{1,0:T(8,128)(2,1)S(1)}, bf16[64,512]{1,0:T(8,128)(2,1)S(1)}, u32[]{:S(2)}, u32[]{:S(2)}) %collective-permute-start.108) | collective-permute-done | bytes 65568 | tf_op jit(solution)/shard_map/ppermute | solution.py:269
  9.5 0.0 copy-start
  9.6 0.1 collective-permute-start.111
  10.3 0.9 %collective-permute-done.111.kv_other = bf16[256,512]{1,0:T(8,128)(2,1)S(1)} collective-permute-done((bf16[256,512]{1,0:T(8,128)(2,1)S(1)}, bf16[256,512]{1,0:T(8,128)(2,1)S(1)}, u32[]{:S(2)}, u32[]{:S(2)}) %collective-permute-start.111) | collective-permute-done | bytes 262176 | tf_op jit(solution)/shard_map/ppermute | solution.py:272
  11.2 0.0 copy-done
  11.2 1.2 %attention.1 = bf16[64,64,128]{2,1,0:T(8,128)(2,1)S(1)} custom-call(s32[17]{0:T(128)S(1)} %get-tuple-element.212.send, s32[2,64]{1,0:T(2,128)S(1)} %get-tuple-element.213.bits, bf16[256,512]{1,0:T(8,128)(2,1)S(1)} %constant_dynamic-update-slice_fusion.kv_own, bf16[256,512]{1,0:T(8,128)(2,1)S(1)} %collective-permute-done.111.kv_other, ...), custom_call_target="tpu_custom_call" | custom-call | tf_op jit(solution)/shard_map/attention/pallas_call | solution.py:274
  12.4 14.9 %conditional.1 = (bf16[64,2048]{1,0:T(8,128)(2,1)}) conditional(s32[]{:T(128)} %bitcast.2, (bf16[64,64,128]{2,1,0:T(8,128)(2,1)S(1)}, s32[68]{0:T(128)S(1)}) %tuple.88, (bf16[64,64,128]{2,1,0:T(8,128)(2,1)S(1)}, s32[68]{0:T(128)S(1)}) %tuple.88, (bf16[64,64,128]{2,1,0:T(8,128)(2,1)S(1)}, s32[68]{0:T(128)S(1)}) %tuple.88, ...), branch_computations={%region_0.1_spmd, %region_1.2_spmd, %region_2.3_spmd, %region_3.4_... | conditional | flops 9 | bytes 6291745 | solution.py:284
  12.6 1.6 %collective-permute-start.51 = (bf16[6,64,128]{2,1,0:T(8,128)(2,1)S(1)}, bf16[6,64,128]{2,1,0:T(8,128)(2,1)S(1)}, u32[]{:S(2)}, u32[]{:S(2)}) collective-permute-start(bf16[6,64,128]{2,1,0:T(8,128)(2,1)S(1)} %get-tuple-element.268), channel_id=1, source_target_pairs={{0,1},{1,0},{2,3},{3,2},{4,6},{5,7},{6,4},{7,5},{8,9},{9,8},{10,11... | collective-permute-start | bytes 294920 | tf_op jit(solution)/shard_map/cond/branch_12_fun/ppermute | solution.py:225
  14.2 0.4 %collective-permute-start.50 = (bf16[6,64,128]{2,1,0:T(8,128)(2,1)S(1)}, bf16[6,64,128]{2,1,0:T(8,128)(2,1)S(1)}, u32[]{:S(2)}, u32[]{:S(2)}) collective-permute-start(bf16[6,64,128]{2,1,0:T(8,128)(2,1)S(1)} %get-tuple-element.269), channel_id=1, source_target_pairs={{0,1},{1,0},{2,3},{3,2},{4,7},{5,6},{6,5},{7,4},{8,9},{9,8},{10,11... | collective-permute-start | bytes 294920 | tf_op jit(solution)/shard_map/cond/branch_12_fun/ppermute | solution.py:225
  14.6 2.6 %collective-permute-start.49 = (bf16[6,64,128]{2,1,0:T(8,128)(2,1)S(1)}, bf16[6,64,128]{2,1,0:T(8,128)(2,1)S(1)}, u32[]{:S(2)}, u32[]{:S(2)}) collective-permute-start(bf16[6,64,128]{2,1,0:T(8,128)(2,1)S(1)} %get-tuple-element.270), channel_id=1, source_target_pairs={{0,2},{1,3},{2,0},{3,1},{4,5},{5,4},{6,7},{7,6},{8,10},{9,11},{10,... | collective-permute-start | bytes 294920 | tf_op jit(solution)/shard_map/cond/branch_12_fun/ppermute | solution.py:225
  17.2 1.4 %collective-permute-start.48 = (bf16[6,64,128]{2,1,0:T(8,128)(2,1)S(1)}, bf16[6,64,128]{2,1,0:T(8,128)(2,1)S(1)}, u32[]{:S(2)}, u32[]{:S(2)}) collective-permute-start(bf16[6,64,128]{2,1,0:T(8,128)(2,1)S(1)} %get-tuple-element.271), channel_id=1, source_target_pairs={{0,3},{1,2},{2,1},{3,0},{4,5},{5,4},{6,7},{7,6},{8,11},{9,10},{10,... | collective-permute-start | bytes 294920 | tf_op jit(solution)/shard_map/cond/branch_12_fun/ppermute | solution.py:225
  18.6 0.0 collective-permute-done.51.refs_4_
  18.6 3.4 %collective-permute-done.50.refs_3_ = bf16[6,64,128]{2,1,0:T(8,128)(2,1)S(1)} collective-permute-done((bf16[6,64,128]{2,1,0:T(8,128)(2,1)S(1)}, bf16[6,64,128]{2,1,0:T(8,128)(2,1)S(1)}, u32[]{:S(2)}, u32[]{:S(2)}) %collective-permute-start.50) | collective-permute-done | bytes 98336 | tf_op jit(solution)/shard_map/cond/branch_12_fun/ppermute | solution.py:225
  22.0 0.0 collective-permute-done.49.refs_2_
  22.0 3.8 %collective-permute-done.48.refs_1_ = bf16[6,64,128]{2,1,0:T(8,128)(2,1)S(1)} collective-permute-done((bf16[6,64,128]{2,1,0:T(8,128)(2,1)S(1)}, bf16[6,64,128]{2,1,0:T(8,128)(2,1)S(1)}, u32[]{:S(2)}, u32[]{:S(2)}) %collective-permute-start.48) | collective-permute-done | bytes 98336 | tf_op jit(solution)/shard_map/cond/branch_12_fun/ppermute | solution.py:225
  25.8 1.3 %place.39 = bf16[64,2048]{1,0:T(8,128)(2,1)} custom-call(s32[68]{0:T(128)S(1)} %get-tuple-element.164.slots, bf16[64,64,128]{2,1,0:T(8,128)(2,1)S(1)} %get-tuple-element.166.refs_0_, bf16[6,64,128]{2,1,0:T(8,128)(2,1)S(1)} %collective-permute-done.48.refs_1_, bf16[6,64,128]{2,1,0:T(8,128)(2,1)S(1)} %collective-permute-done.49.refs_2_, ...), custom_call_target="tpu_custom_call" | custom-call | tf_op jit(solution)/shard_map/cond/branch_12_fun/place/pallas_call | solution.py:227
  (6 shorter events, 0.1 us)
Async XLA Ops:
  0.8 4.6 %copy-start.1 = (s32[64,8]{0,1:T(8,128)S(1)}, s32[64,8]{0,1:T(8,128)}, u32[]{:S(2)}) copy-start(s32[64,8]{0,1:T(8,128)} %param.36) | copy-start | bytes 6148
  0.8 4.6 %copy-start.2 = (s32[64,8]{0,1:T(8,128)S(1)}, s32[64,8]{0,1:T(8,128)}, u32[]{:S(2)}) copy-start(s32[64,8]{0,1:T(8,128)} %param.37) | copy-start | bytes 6148
  0.8 6.7 %collective-permute-start.110 = (bf16[64,512]{1,0:T(8,128)(2,1)S(1)}, bf16[64,512]{1,0:T(8,128)(2,1)S(1)}, u32[]{:S(2)}, u32[]{:S(2)}) collective-permute-start(bf16[64,512]{1,0:T(8,128)(2,1)S(1)} %pad_maximum_fusion), channel_id=1, source_target_pairs={{0,24},{4,28},{8,16},{12,20},{16,8},{20,12},{24,0},{28,4},{1,25},{... | collective-permute-start | bytes 196616 | tf_op jit(solution)/shard_map/ppermute | solution.py:269
  4.8 4.3 %collective-permute-start.109 = (bf16[64,512]{1,0:T(8,128)(2,1)S(1)}, bf16[64,512]{1,0:T(8,128)(2,1)S(1)}, u32[]{:S(2)}, u32[]{:S(2)}) collective-permute-start(bf16[64,512]{1,0:T(8,128)(2,1)S(1)} %pad_maximum_fusion), channel_id=1, source_target_pairs={{0,16},{4,12},{8,24},{12,4},{16,0},{20,28},{24,8},{28,20},{1,17},{... | collective-permute-start | bytes 196616 | tf_op jit(solution)/shard_map/ppermute | solution.py:269
  5.3 4.3 %collective-permute-start.108 = (bf16[64,512]{1,0:T(8,128)(2,1)S(1)}, bf16[64,512]{1,0:T(8,128)(2,1)S(1)}, u32[]{:S(2)}, u32[]{:S(2)}) collective-permute-start(bf16[64,512]{1,0:T(8,128)(2,1)S(1)} %pad_maximum_fusion), channel_id=1, source_target_pairs={{0,8},{4,20},{8,0},{12,28},{16,24},{20,4},{24,16},{28,12},{1,9},{5... | collective-permute-start | bytes 196616 | tf_op jit(solution)/shard_map/ppermute | solution.py:269
  5.4 0.7 %copy-start.3 = (s32[64]{0:T(128)S(1)}, s32[64]{0:T(128)}, u32[]{:S(2)}) copy-start(s32[64]{0:T(128)} %plan.1) | copy-start | bytes 772
  9.5 1.7 %copy-start = (bf16[64,2048]{1,0:T(8,128)(2,1)S(1)}, bf16[64,2048]{1,0:T(8,128)(2,1)}, u32[]{:S(2)}) copy-start(bf16[64,2048]{1,0:T(8,128)(2,1)} %query_ref.1) | copy-start | bytes 786436
  9.6 1.6 %collective-permute-start.111 = (bf16[256,512]{1,0:T(8,128)(2,1)S(1)}, bf16[256,512]{1,0:T(8,128)(2,1)S(1)}, u32[]{:S(2)}, u32[]{:S(2)}) collective-permute-start(bf16[256,512]{1,0:T(8,128)(2,1)S(1)} %constant_dynamic-update-slice_fusion.kv_own), channel_id=1, source_target_pairs={{0,4},{4,0},{8,12},{12,8},{16,20},{20,16},{24,28},{28,24},{1,5},{5... | collective-permute-start | bytes 786440 | tf_op jit(solution)/shard_map/ppermute | solution.py:272
  12.6 6.0 %collective-permute-start.51 = (bf16[6,64,128]{2,1,0:T(8,128)(2,1)S(1)}, bf16[6,64,128]{2,1,0:T(8,128)(2,1)S(1)}, u32[]{:S(2)}, u32[]{:S(2)}) collective-permute-start(bf16[6,64,128]{2,1,0:T(8,128)(2,1)S(1)} %get-tuple-element.268), channel_id=1, source_target_pairs={{0,1},{1,0},{2,3},{3,2},{4,6},{5,7},{6,4},{7,5},{8,9},{9,8},{10,11... | collective-permute-start | bytes 294920 | tf_op jit(solution)/shard_map/cond/branch_12_fun/ppermute | solution.py:225
  14.2 7.8 %collective-permute-start.50 = (bf16[6,64,128]{2,1,0:T(8,128)(2,1)S(1)}, bf16[6,64,128]{2,1,0:T(8,128)(2,1)S(1)}, u32[]{:S(2)}, u32[]{:S(2)}) collective-permute-start(bf16[6,64,128]{2,1,0:T(8,128)(2,1)S(1)} %get-tuple-element.269), channel_id=1, source_target_pairs={{0,1},{1,0},{2,3},{3,2},{4,7},{5,6},{6,5},{7,4},{8,9},{9,8},{10,11... | collective-permute-start | bytes 294920 | tf_op jit(solution)/shard_map/cond/branch_12_fun/ppermute | solution.py:225
  14.6 7.3 %collective-permute-start.49 = (bf16[6,64,128]{2,1,0:T(8,128)(2,1)S(1)}, bf16[6,64,128]{2,1,0:T(8,128)(2,1)S(1)}, u32[]{:S(2)}, u32[]{:S(2)}) collective-permute-start(bf16[6,64,128]{2,1,0:T(8,128)(2,1)S(1)} %get-tuple-element.270), channel_id=1, source_target_pairs={{0,2},{1,3},{2,0},{3,1},{4,5},{5,4},{6,7},{7,6},{8,10},{9,11},{10,... | collective-permute-start | bytes 294920 | tf_op jit(solution)/shard_map/cond/branch_12_fun/ppermute | solution.py:225
  17.2 8.5 %collective-permute-start.48 = (bf16[6,64,128]{2,1,0:T(8,128)(2,1)S(1)}, bf16[6,64,128]{2,1,0:T(8,128)(2,1)S(1)}, u32[]{:S(2)}, u32[]{:S(2)}) collective-permute-start(bf16[6,64,128]{2,1,0:T(8,128)(2,1)S(1)} %get-tuple-element.271), channel_id=1, source_target_pairs={{0,3},{1,2},{2,1},{3,0},{4,5},{5,4},{6,7},{7,6},{8,11},{9,10},{10,... | collective-permute-start | bytes 294920 | tf_op jit(solution)/shard_map/cond/branch_12_fun/ppermute | solution.py:225
where the time goes:
time: 27.3 us; the launch traced here: 27.5 us
  starting transfers between devices  10.7 us (39%)
  waiting for transfers between devices  10 us (37%)
  Pallas kernels  4.01 us (15%)
  local copies, waits for them, and re-layouts  1.5 us (5%)
  between operations  0.91 us (3%)
  loops' own time  0.32 us (1%)
    ppermute x4, waiting for transfers between devices, exchange(): arrived.append(lax.ppermute(heads, ('seq', 'head'), pairs))  7.19 us
    ppermute x4, starting transfers between devices, exchange(): arrived.append(lax.ppermute(heads, ('seq', 'head'), pairs))  6.03 us
    ppermute x3, starting transfers between devices, per_device(): lax.ppermute(kv, 'seq', [(i, i ^ flips[i & 1]) for i in range(seq_size)])  4.6 us
    ppermute x3, waiting for transfers between devices, per_device(): lax.ppermute(kv, 'seq', [(i, i ^ flips[i & 1]) for i in range(seq_size)])  1.98 us
    pallas_call x1, Pallas kernels, per_device(): pl.pallas_call(functools.partial(route_kernel, head_size, held, levels),...  1.47 us
    pallas_call x1, Pallas kernels, exchange(): pl.pallas_call(functools.partial(place_kernel, head_size, held, [kept] +...  1.31 us
    pallas_call x1, Pallas kernels, per_device(): pl.pallas_call(functools.partial(attention_kernel, seq_size, held, kv_hea...  1.23 us
    ppermute x1, waiting for transfers between devices, per_device(): lax.ppermute(kv_own, 'seq', [(i, i ^ 1) for i in range(seq_size)])  0.87 us
  transfers between devices with their start and end apart: 8, of which 5 were waited for; matrix products, arithmetic and copies ran while one was open for 0% of the time, Pallas kernels for 5%

commit v1 on v0

--- a/solution.py
+++ b/solution.py
@@ -27,10 +27,6 @@
 def shift_of(size):
     assert size & (size - 1) == 0
     return size.bit_length() - 1
-
-
-def turned(index, size):
-    return ((index << 1) | (index >> (shift_of(size) - 1))) & (size - 1)
 
 
 def entry_bits(table):
@@ -114,9 +110,7 @@
 
     piece = lax.broadcasted_iota(jnp.int32, (1, 2 * half), 1) // key_len
     core = jnp.where(piece < chips, own_seq & 1, 1 - (own_seq & 1))
-    flip = piece & (chips - 1)
-    flip = jnp.where(core == 0, flip, turned(flip, chips))
-    block = ((own_seq >> 1) ^ flip) * 2 + core
+    block = ((own_seq >> 1) ^ (piece & (chips - 1))) * 2 + core
     back = own_seq - block
     present = back >= 0
     back_shift = jnp.maximum(back, 0)
@@ -206,7 +200,7 @@
     b, c = capacities[2:]
     near, rest = (1, 0, 0), (1, min(b, held - c), b)
     middle, far = (2, 0, 0), (3, 0, 0)
-    return [(c, (far, rest)), (b, (middle, near)), (c, (rest, far)), (b, (near, middle))]
+    return [(c, (rest, far)), (b, (near, middle)), (c, (far, rest)), (b, (middle, near))]
 
 
 def exchange(head_size, held, capacities, packed, slots):
@@ -265,8 +259,7 @@
     )
     pieces = [kv]
     for m in range(1, chips):
-        flips = (2 * m, 2 * turned(m, chips))
-        pieces.append(lax.ppermute(kv, "seq", [(i, i ^ flips[i & 1]) for i in range(seq_size)]))
+        pieces.append(lax.ppermute(kv, "seq", [(i, i ^ (2 * m)) for i in range(seq_size)]))
     pieces, send, slots, level, bits = lax.optimization_barrier((pieces, send, slots, level, bits))
     kv_own = jnp.concatenate(pieces, axis=0)
     kv_other = lax.ppermute(kv_own, "seq", [(i, i ^ 1) for i in range(seq_size)])

time: 27.3 us -> 25.8 us (0.945); the launches traced: 27.5 us -> 25.3 us
  waiting for transfers between devices: 10 us -> 7.9 us
    ppermute x4, waiting for transfers between devices: 7.19 us -> 5.05 us  [exchange(): arrived.append(lax.ppermute(heads, ('seq', 'head'), pairs))]
  transfers between devices with their start and end apart: 8 -> 8, of which waited for: 5 -> 6; matrix products, arithmetic and copies ran while one was open for 0% -> 0% of each run, Pallas kernels for 5% -> 6%
where the time goes in v1:
time: 25.8 us; the launch traced here: 25.3 us
  starting transfers between devices  10.7 us (41%)
  waiting for transfers between devices  7.9 us (31%)
  Pallas kernels  4 us (16%)
  local copies, waits for them, and re-layouts  1.5 us (6%)
  between operations  0.91 us (4%)
  loops' own time  0.32 us (1%)
    ppermute x4, starting transfers between devices, exchange(): arrived.append(lax.ppermute(heads, ('seq', 'head'), pairs))  6.03 us
    ppermute x4, waiting for transfers between devices, exchange(): arrived.append(lax.ppermute(heads, ('seq', 'head'), pairs))  5.05 us
    ppermute x3, starting transfers between devices, per_device(): lax.ppermute(kv, 'seq', [(i, i ^ 2 * m) for i in range(seq_size)])  4.6 us
    ppermute x3, waiting for transfers between devices, per_device(): lax.ppermute(kv, 'seq', [(i, i ^ 2 * m) for i in range(seq_size)])  1.98 us
    pallas_call x1, Pallas kernels, per_device(): pl.pallas_call(functools.partial(route_kernel, head_size, held, levels),...  1.47 us
    pallas_call x1, Pallas kernels, exchange(): pl.pallas_call(functools.partial(place_kernel, head_size, held, [kept] +...  1.3 us
    pallas_call x1, Pallas kernels, per_device(): pl.pallas_call(functools.partial(attention_kernel, seq_size, held, kv_hea...  1.23 us
    ppermute x1, waiting for transfers between devices, per_device(): lax.ppermute(kv_own, 'seq', [(i, i ^ 1) for i in range(seq_size)])  0.87 us
  transfers between devices with their start and end apart: 8, of which 6 were waited for; matrix products, arithmetic and copies ran while one was open for 0% of the time, Pallas kernels for 6%

profile of v1, /device:TPU:0, one launch (start us, length us, event | category | flops | bytes accessed | tf_op | source)
XLA Modules:
  0.0 25.3 jit_solution(14097290974009504533)
XLA Ops:
  0.0 0.8 %constant_dynamic-slice_fusion.108 = (bf16[64,256]{1,0:T(8,128)(2,1)S(1)}, bf16[64,256]{1,0:T(8,128)(2,1)S(1)}) fusion(bf16[64,1024]{1,0:T(8,128)(2,1)} %param.35, s32[]{:T(128)S(6)} %select_n.443, bf16[64,1024]{1,0:T(8,128)(2,1)} %param.34), kind=kLoop, calls=%fused_computation.113 | loop fusion | bytes 131076 | tf_op jit(solution)/shard_map/dynamic_slice | solution.py:258
  0.8 0.0 copy-start.1
  0.8 0.0 copy-start.2
  0.8 4.0 %collective-permute-start.110 = (bf16[64,512]{1,0:T(8,128)(2,1)S(1)}, bf16[64,512]{1,0:T(8,128)(2,1)S(1)}, u32[]{:S(2)}, u32[]{:S(2)}) collective-permute-start(bf16[64,512]{1,0:T(8,128)(2,1)S(1)} %pad_maximum_fusion), channel_id=1, source_target_pairs={{0,24},{4,28},{8,16},{12,20},{16,8},{20,12},{24,0},{28,4},{1,25},{... | collective-permute-start | bytes 196616 | tf_op jit(solution)/shard_map/ppermute | solution.py:262
  4.8 0.5 %collective-permute-start.109 = (bf16[64,512]{1,0:T(8,128)(2,1)S(1)}, bf16[64,512]{1,0:T(8,128)(2,1)S(1)}, u32[]{:S(2)}, u32[]{:S(2)}) collective-permute-start(bf16[64,512]{1,0:T(8,128)(2,1)S(1)} %pad_maximum_fusion), channel_id=1, source_target_pairs={{0,16},{4,20},{8,24},{12,28},{16,0},{20,4},{24,8},{28,12},{1,17},{... | collective-permute-start | bytes 196616 | tf_op jit(solution)/shard_map/ppermute | solution.py:262
  5.3 0.1 collective-permute-start.108
  5.4 0.0 copy-start.3
  5.4 0.0 copy-done.1
  5.4 0.0 copy-done.2
  5.4 0.6 %copy-done.3 = s32[64]{0:T(128)S(1)} copy-done((s32[64]{0:T(128)S(1)}, s32[64]{0:T(128)}, u32[]{:S(2)}) %copy-start.3) | copy-done | bytes 280
  6.1 1.5 %route.1 = (s32[17]{0:T(128)S(1)}, s32[68]{0:T(128)S(1)}, s32[1]{0:T(128)}, s32[2,64]{1,0:T(2,128)S(1)}) custom-call(s32[64]{0:T(128)S(1)} %copy-done.3, s32[8,64]{1,0:T(8,128)S(1)} %bitcast.3, s32[8,64]{1,0:T(8,128)S(1)} %bitcast.4), custom_call_target="tpu_custom_call" | custom-call | tf_op jit(solution)/shard_map/route/pallas_call | solution.py:242
  7.5 0.0 collective-permute-done.110
  7.6 1.5 %collective-permute-done.109 = bf16[64,512]{1,0:T(8,128)(2,1)S(1)} collective-permute-done((bf16[64,512]{1,0:T(8,128)(2,1)S(1)}, bf16[64,512]{1,0:T(8,128)(2,1)S(1)}, u32[]{:S(2)}, u32[]{:S(2)}) %collective-permute-start.109) | collective-permute-done | bytes 65568 | tf_op jit(solution)/shard_map/ppermute | solution.py:262
  9.0 0.5 %collective-permute-done.108 = bf16[64,512]{1,0:T(8,128)(2,1)S(1)} collective-permute-done((bf16[64,512]{1,0:T(8,128)(2,1)S(1)}, bf16[64,512]{1,0:T(8,128)(2,1)S(1)}, u32[]{:S(2)}, u32[]{:S(2)}) %collective-permute-start.108) | collective-permute-done | bytes 65568 | tf_op jit(solution)/shard_map/ppermute | solution.py:262
  9.5 0.0 copy-start
  9.6 0.1 collective-permute-start.111
  10.3 0.9 %collective-permute-done.111.kv_other = bf16[256,512]{1,0:T(8,128)(2,1)S(1)} collective-permute-done((bf16[256,512]{1,0:T(8,128)(2,1)S(1)}, bf16[256,512]{1,0:T(8,128)(2,1)S(1)}, u32[]{:S(2)}, u32[]{:S(2)}) %collective-permute-start.111) | collective-permute-done | bytes 262176 | tf_op jit(solution)/shard_map/ppermute | solution.py:265
  11.2 0.0 copy-done
  11.2 1.2 %attention.1 = bf16[64,64,128]{2,1,0:T(8,128)(2,1)S(1)} custom-call(s32[17]{0:T(128)S(1)} %get-tuple-element.212.send, s32[2,64]{1,0:T(2,128)S(1)} %get-tuple-element.213.bits, bf16[256,512]{1,0:T(8,128)(2,1)S(1)} %constant_dynamic-update-slice_fusion.kv_own, bf16[256,512]{1,0:T(8,128)(2,1)S(1)} %collective-permute-done.111.kv_other, ...), custom_call_target="tpu_custom_call" | custom-call | tf_op jit(solution)/shard_map/attention/pallas_call | solution.py:267
  12.4 12.7 %conditional.1 = (bf16[64,2048]{1,0:T(8,128)(2,1)}) conditional(s32[]{:T(128)} %bitcast.2, (bf16[64,64,128]{2,1,0:T(8,128)(2,1)S(1)}, s32[68]{0:T(128)S(1)}) %tuple.88, (bf16[64,64,128]{2,1,0:T(8,128)(2,1)S(1)}, s32[68]{0:T(128)S(1)}) %tuple.88, (bf16[64,64,128]{2,1,0:T(8,128)(2,1)S(1)}, s32[68]{0:T(128)S(1)}) %tuple.88, ...), branch_computations={%region_0.1_spmd, %region_1.2_spmd, %region_2.3_spmd, %region_3.4_... | conditional | flops 9 | bytes 6291745 | solution.py:277
  12.5 2.7 %collective-permute-start.19 = (bf16[5,64,128]{2,1,0:T(8,128)(2,1)S(1)}, bf16[5,64,128]{2,1,0:T(8,128)(2,1)S(1)}, u32[]{:S(2)}, u32[]{:S(2)}) collective-permute-start(bf16[5,64,128]{2,1,0:T(8,128)(2,1)S(1)} %get-tuple-element.236), channel_id=1, source_target_pairs={{0,2},{1,3},{2,0},{3,1},{4,5},{5,4},{6,7},{7,6},{8,10},{9,11},{10,... | collective-permute-start | bytes 245768 | tf_op jit(solution)/shard_map/cond/branch_4_fun/ppermute | solution.py:219
  15.2 1.4 %collective-permute-start.18 = (bf16[5,64,128]{2,1,0:T(8,128)(2,1)S(1)}, bf16[5,64,128]{2,1,0:T(8,128)(2,1)S(1)}, u32[]{:S(2)}, u32[]{:S(2)}) collective-permute-start(bf16[5,64,128]{2,1,0:T(8,128)(2,1)S(1)} %get-tuple-element.237), channel_id=1, source_target_pairs={{0,3},{1,2},{2,1},{3,0},{4,5},{5,4},{6,7},{7,6},{8,11},{9,10},{10,... | collective-permute-start | bytes 245768 | tf_op jit(solution)/shard_map/cond/branch_4_fun/ppermute | solution.py:219
  16.5 0.2 collective-permute-start.17
  16.8 1.8 %collective-permute-start.16 = (bf16[5,64,128]{2,1,0:T(8,128)(2,1)S(1)}, bf16[5,64,128]{2,1,0:T(8,128)(2,1)S(1)}, u32[]{:S(2)}, u32[]{:S(2)}) collective-permute-start(bf16[5,64,128]{2,1,0:T(8,128)(2,1)S(1)} %get-tuple-element.239), channel_id=1, source_target_pairs={{0,1},{1,0},{2,3},{3,2},{4,7},{5,6},{6,5},{7,4},{8,9},{9,8},{10,11... | collective-permute-start | bytes 245768 | tf_op jit(solution)/shard_map/cond/branch_4_fun/ppermute | solution.py:219
  18.6 0.1 collective-permute-done.19.refs_4_
  18.7 3.8 %collective-permute-done.18.refs_3_ = bf16[5,64,128]{2,1,0:T(8,128)(2,1)S(1)} collective-permute-done((bf16[5,64,128]{2,1,0:T(8,128)(2,1)S(1)}, bf16[5,64,128]{2,1,0:T(8,128)(2,1)S(1)}, u32[]{:S(2)}, u32[]{:S(2)}) %collective-permute-start.18) | collective-permute-done | bytes 81952 | tf_op jit(solution)/shard_map/cond/branch_4_fun/ppermute | solution.py:219
  22.5 0.0 collective-permute-done.17.refs_2_
  22.5 1.1 %collective-permute-done.16.refs_1_ = bf16[5,64,128]{2,1,0:T(8,128)(2,1)S(1)} collective-permute-done((bf16[5,64,128]{2,1,0:T(8,128)(2,1)S(1)}, bf16[5,64,128]{2,1,0:T(8,128)(2,1)S(1)}, u32[]{:S(2)}, u32[]{:S(2)}) %collective-permute-start.16) | collective-permute-done | bytes 81952 | tf_op jit(solution)/shard_map/cond/branch_4_fun/ppermute | solution.py:219
  23.6 1.3 %place.31 = bf16[64,2048]{1,0:T(8,128)(2,1)} custom-call(s32[68]{0:T(128)S(1)} %get-tuple-element.132.slots, bf16[64,64,128]{2,1,0:T(8,128)(2,1)S(1)} %get-tuple-element.133.refs_0_, bf16[5,64,128]{2,1,0:T(8,128)(2,1)S(1)} %collective-permute-done.16.refs_1_, bf16[5,64,128]{2,1,0:T(8,128)(2,1)S(1)} %collective-permute-done.17.refs_2_, ...), custom_call_target="tpu_custom_call" | custom-call | tf_op jit(solution)/shard_map/cond/branch_4_fun/place/pallas_call | solution.py:221
  (6 shorter events, 0.1 us)
Async XLA Ops:
  0.8 4.6 %copy-start.1 = (s32[64,8]{0,1:T(8,128)S(1)}, s32[64,8]{0,1:T(8,128)}, u32[]{:S(2)}) copy-start(s32[64,8]{0,1:T(8,128)} %param.36) | copy-start | bytes 6148
  0.8 4.6 %copy-start.2 = (s32[64,8]{0,1:T(8,128)S(1)}, s32[64,8]{0,1:T(8,128)}, u32[]{:S(2)}) copy-start(s32[64,8]{0,1:T(8,128)} %param.37) | copy-start | bytes 6148
  0.8 6.7 %collective-permute-start.110 = (bf16[64,512]{1,0:T(8,128)(2,1)S(1)}, bf16[64,512]{1,0:T(8,128)(2,1)S(1)}, u32[]{:S(2)}, u32[]{:S(2)}) collective-permute-start(bf16[64,512]{1,0:T(8,128)(2,1)S(1)} %pad_maximum_fusion), channel_id=1, source_target_pairs={{0,24},{4,28},{8,16},{12,20},{16,8},{20,12},{24,0},{28,4},{1,25},{... | collective-permute-start | bytes 196616 | tf_op jit(solution)/shard_map/ppermute | solution.py:262
  4.8 4.3 %collective-permute-start.109 = (bf16[64,512]{1,0:T(8,128)(2,1)S(1)}, bf16[64,512]{1,0:T(8,128)(2,1)S(1)}, u32[]{:S(2)}, u32[]{:S(2)}) collective-permute-start(bf16[64,512]{1,0:T(8,128)(2,1)S(1)} %pad_maximum_fusion), channel_id=1, source_target_pairs={{0,16},{4,20},{8,24},{12,28},{16,0},{20,4},{24,8},{28,12},{1,17},{... | collective-permute-start | bytes 196616 | tf_op jit(solution)/shard_map/ppermute | solution.py:262
  5.3 4.3 %collective-permute-start.108 = (bf16[64,512]{1,0:T(8,128)(2,1)S(1)}, bf16[64,512]{1,0:T(8,128)(2,1)S(1)}, u32[]{:S(2)}, u32[]{:S(2)}) collective-permute-start(bf16[64,512]{1,0:T(8,128)(2,1)S(1)} %pad_maximum_fusion), channel_id=1, source_target_pairs={{0,8},{4,12},{8,0},{12,4},{16,24},{20,28},{24,16},{28,20},{1,9},{5... | collective-permute-start | bytes 196616 | tf_op jit(solution)/shard_map/ppermute | solution.py:262
  5.4 0.7 %copy-start.3 = (s32[64]{0:T(128)S(1)}, s32[64]{0:T(128)}, u32[]{:S(2)}) copy-start(s32[64]{0:T(128)} %plan.1) | copy-start | bytes 772
  9.5 1.7 %copy-start = (bf16[64,2048]{1,0:T(8,128)(2,1)S(1)}, bf16[64,2048]{1,0:T(8,128)(2,1)}, u32[]{:S(2)}) copy-start(bf16[64,2048]{1,0:T(8,128)(2,1)} %query_ref.1) | copy-start | bytes 786436
  9.6 1.6 %collective-permute-start.111 = (bf16[256,512]{1,0:T(8,128)(2,1)S(1)}, bf16[256,512]{1,0:T(8,128)(2,1)S(1)}, u32[]{:S(2)}, u32[]{:S(2)}) collective-permute-start(bf16[256,512]{1,0:T(8,128)(2,1)S(1)} %constant_dynamic-update-slice_fusion.kv_own), channel_id=1, source_target_pairs={{0,4},{4,0},{8,12},{12,8},{16,20},{20,16},{24,28},{28,24},{1,5},{5... | collective-permute-start | bytes 786440 | tf_op jit(solution)/shard_map/ppermute | solution.py:265
  12.5 6.2 %collective-permute-start.19 = (bf16[5,64,128]{2,1,0:T(8,128)(2,1)S(1)}, bf16[5,64,128]{2,1,0:T(8,128)(2,1)S(1)}, u32[]{:S(2)}, u32[]{:S(2)}) collective-permute-start(bf16[5,64,128]{2,1,0:T(8,128)(2,1)S(1)} %get-tuple-element.236), channel_id=1, source_target_pairs={{0,2},{1,3},{2,0},{3,1},{4,5},{5,4},{6,7},{7,6},{8,10},{9,11},{10,... | collective-permute-start | bytes 245768 | tf_op jit(solution)/shard_map/cond/branch_4_fun/ppermute | solution.py:219
  15.2 7.3 %collective-permute-start.18 = (bf16[5,64,128]{2,1,0:T(8,128)(2,1)S(1)}, bf16[5,64,128]{2,1,0:T(8,128)(2,1)S(1)}, u32[]{:S(2)}, u32[]{:S(2)}) collective-permute-start(bf16[5,64,128]{2,1,0:T(8,128)(2,1)S(1)} %get-tuple-element.237), channel_id=1, source_target_pairs={{0,3},{1,2},{2,1},{3,0},{4,5},{5,4},{6,7},{7,6},{8,11},{9,10},{10,... | collective-permute-start | bytes 245768 | tf_op jit(solution)/shard_map/cond/branch_4_fun/ppermute | solution.py:219
  16.5 6.0 %collective-permute-start.17 = (bf16[5,64,128]{2,1,0:T(8,128)(2,1)S(1)}, bf16[5,64,128]{2,1,0:T(8,128)(2,1)S(1)}, u32[]{:S(2)}, u32[]{:S(2)}) collective-permute-start(bf16[5,64,128]{2,1,0:T(8,128)(2,1)S(1)} %get-tuple-element.238), channel_id=1, source_target_pairs={{0,1},{1,0},{2,3},{3,2},{4,6},{5,7},{6,4},{7,5},{8,9},{9,8},{10,11... | collective-permute-start | bytes 245768 | tf_op jit(solution)/shard_map/cond/branch_4_fun/ppermute | solution.py:219
  16.8 6.8 %collective-permute-start.16 = (bf16[5,64,128]{2,1,0:T(8,128)(2,1)S(1)}, bf16[5,64,128]{2,1,0:T(8,128)(2,1)S(1)}, u32[]{:S(2)}, u32[]{:S(2)}) collective-permute-start(bf16[5,64,128]{2,1,0:T(8,128)(2,1)S(1)} %get-tuple-element.239), channel_id=1, source_target_pairs={{0,1},{1,0},{2,3},{3,2},{4,7},{5,6},{6,5},{7,4},{8,9},{9,8},{10,11... | collective-permute-start | bytes 245768 | tf_op jit(solution)/shard_map/cond/branch_4_fun/ppermute | solution.py:219
